TPU v7x, 256 devices: a whole 4x4x8 slice. The times are simulated.
256 devices in a mesh: dp: 32 (over x, z), seq: 8 (over y, core).
Axes of the slice: x: 4, y: 4, z: 8, core: 2. Of those that a mesh axis runs over, the one named last changes fastest.
Arguments:
- pixels: bfloat16 [32768, 1176], P(('dp', 'seq')), may hold values from -6 to 6
- patch_weight: bfloat16 [1176, 1280], replicated, may hold values from -0.1875 to 0.1875
- ln_gain: float32 [1280], replicated, may hold values from 0.1 to 1.9
- ln_bias: float32 [1280], replicated, may hold values from -1.5 to 1.5
- qkv_weight: bfloat16 [1280, 3840], P('dp'), may hold values from -4 to 4
- qkv_bias: float32 [3840], replicated, may hold values from -2.5 to 2.5
- out_weight: bfloat16 [1280, 1280], P('dp'), may hold values from -0.15625 to 0.15625
- out_bias: float32 [1280], replicated, may hold values from -1.5 to 1.5
- offsets: int32 [32, 3], P('dp'), may hold values from 0 to 854, as said below
- widths: int32 [32, 3], P('dp'), may hold values from 16 to 64
Outputs:
- encoded: bfloat16 [32768, 1280], P(('dp', 'seq'))
Inputs may be any that keep to these rules, and one draw needn't show every extreme that they name: In every group the first offset is 0 and offsets rise; every image holds 170 or more tokens and the last image ends at position 1024; in some group the last image holds exactly 170 tokens.
All inputs are finite; a program needn't handle non-finite values.
Results may differ from a plain program's by a relative error of at most 0.012.
Values may be sent and summed in bfloat16 or wider, within the bound.
No kernel may reach another device: no remote copies, remote signals or barrier semaphores. Data moves between devices by JAX's collectives and lax.ppermute only.
A program may use at most 64 MiB of HBM per device.

v0:
```python
import jax
import jax.numpy as jnp
from jax import lax
from jax.sharding import PartitionSpec as P

HEADS = 16
HDIM = 80


def image_lookup(positions, starts):
    return jnp.sum((positions[:, None] >= starts[None, :]).astype(jnp.int32), axis=1) - 1


def rotation_tables(positions, starts, image_widths, head_size):
    image_index = image_lookup(positions, starts)
    onehot = (image_index[:, None] == jnp.arange(starts.shape[0], dtype=jnp.int32)[None, :]).astype(
        jnp.int32
    )
    first_position = jnp.sum(onehot * starts[None, :], axis=1)
    across = jnp.sum(onehot * image_widths[None, :], axis=1)
    within = positions - first_position
    row_index = within // across
    column_index = within - row_index * across
    quarter = head_size // 4
    inverse = 1.0 / 10000.0 ** (jnp.arange(quarter, dtype=jnp.float32) * 2.0 / (head_size // 2))
    angles = jnp.concatenate(
        [
            row_index.astype(jnp.float32)[:, None] * inverse[None, :],
            column_index.astype(jnp.float32)[:, None] * inverse[None, :],
        ],
        axis=1,
    )
    angles = jnp.concatenate([angles, angles], axis=1)
    return (jnp.cos(angles), jnp.sin(angles), image_index)


def rotate_heads(values, cosine, sine_table, head_size):
    half_size = head_size // 2
    turned = jnp.concatenate([-values[..., half_size:], values[..., :half_size]], axis=-1)
    return values * cosine[:, None, :] + turned * sine_table[:, None, :]


def layer_norm(embedded, ln_gain, ln_bias):
    values = embedded.astype(jnp.float32)
    center = values - jnp.mean(values, axis=-1, keepdims=True)
    variance = jnp.mean(center * center, axis=-1, keepdims=True)
    return (center * lax.rsqrt(variance + 1e-06) * ln_gain + ln_bias).astype(jnp.bfloat16)


def block_length(count):
    length = min(count, 512)
    while count % length:
        length -= 1
    return length


def attend_block(state, queries3, key_block, value_block, query_image, key_image, score_scale):
    running_max, running_total, accum = state
    count = key_block.shape[0]
    scores = (
        jnp.einsum(
            "qhd,khd->hqk",
            queries3,
            key_block.reshape(count, HEADS, HDIM),
            preferred_element_type=jnp.float32,
        )
        * score_scale
    )
    allowed = (query_image[:, None] == key_image[None, :])[None]
    scores = jnp.where(allowed, scores, -1e30)
    new_max = jnp.maximum(running_max, jnp.max(scores, axis=-1))
    weights = jnp.where(allowed, jnp.exp(scores - new_max[..., None]), 0.0)
    factor = jnp.exp(running_max - new_max)
    running_total = running_total * factor + jnp.sum(weights, axis=-1)
    part_sum = jnp.einsum(
        "hqk,khd->qhd",
        weights.astype(jnp.bfloat16),
        value_block.reshape(count, HEADS, HDIM),
        preferred_element_type=jnp.float32,
    )
    accum = accum * factor.T[:, :, None] + part_sum
    return (new_max, running_total, accum)


def per_device(
    pixels,
    patch_weight,
    ln_gain,
    ln_bias,
    qkv_weight,
    qkv_bias,
    out_weight,
    out_bias,
    offsets,
    widths,
):
    local_pixels = lax.all_to_all(pixels, "dp", split_axis=0, concat_axis=0, tiled=True)
    tok_rows = local_pixels.shape[0]
    dmodel = patch_weight.shape[1]
    score_scale = HDIM ** (-0.5)
    embedded = jnp.dot(local_pixels, patch_weight, preferred_element_type=jnp.float32).astype(
        jnp.bfloat16
    )
    normed = layer_norm(embedded, ln_gain, ln_bias)
    columns = normed
    projected = (
        jnp.dot(
            columns,
            lax.all_gather(qkv_weight, "dp", axis=0, tiled=True),
            preferred_element_type=jnp.float32,
        )
        + qkv_bias
    )
    starts = offsets[0]
    image_widths = widths[0]
    positions = lax.axis_index("seq") * tok_rows + jnp.arange(tok_rows, dtype=jnp.int32)
    cosine, sine_table, query_image = rotation_tables(positions, starts, image_widths, HDIM)
    queries = (
        rotate_heads(projected[:, :dmodel].reshape(tok_rows, HEADS, HDIM), cosine, sine_table, HDIM)
        .reshape(tok_rows, dmodel)
        .astype(jnp.bfloat16)
    )
    key_rows = (
        rotate_heads(
            projected[:, dmodel : 2 * dmodel].reshape(tok_rows, HEADS, HDIM),
            cosine,
            sine_table,
            HDIM,
        )
        .reshape(tok_rows, dmodel)
        .astype(jnp.bfloat16)
    )
    values = projected[:, 2 * dmodel :].astype(jnp.bfloat16)
    queries3 = queries.reshape(tok_rows, HEADS, HDIM)
    initial = (
        jnp.full((HEADS, tok_rows), -1e30, jnp.float32),
        jnp.zeros((HEADS, tok_rows), jnp.float32),
        jnp.zeros((tok_rows, HEADS, HDIM), jnp.float32),
    )
    piece_keys = lax.all_gather(key_rows, "seq", axis=0, tiled=True)
    piece_values = lax.all_gather(values, "seq", axis=0, tiled=True)
    count = piece_keys.shape[0]
    length = block_length(count)

    def one_block(block_index, inner):
        first_row = block_index * length
        key_block = lax.dynamic_slice_in_dim(piece_keys, first_row, length, 0)
        value_block = lax.dynamic_slice_in_dim(piece_values, first_row, length, 0)
        key_image = image_lookup(first_row + jnp.arange(length, dtype=jnp.int32), starts)
        return attend_block(
            inner, queries3, key_block, value_block, query_image, key_image, score_scale
        )

    final_state = lax.fori_loop(0, count // length, one_block, initial)
    attended = (
        (final_state[2] / final_state[1].T[:, :, None])
        .reshape(tok_rows, dmodel)
        .astype(jnp.bfloat16)
    )
    columns = attended
    mixed = jnp.dot(
        columns,
        lax.all_gather(out_weight, "dp", axis=0, tiled=True),
        preferred_element_type=jnp.float32,
    )
    return (embedded.astype(jnp.float32) + mixed + out_bias).astype(jnp.bfloat16)


def solution(mesh):
    in_specs = (
        P(("dp", "seq"), None),
        P(),
        P(),
        P(),
        P("dp", None),
        P(),
        P("dp", None),
        P(),
        P("dp", None),
        P("dp", None),
    )
    out_specs = P(("dp", "seq"), None)
    return jax.shard_map(
        per_device, mesh=mesh, in_specs=in_specs, out_specs=out_specs, check_vma=False
    )
```

profile of v0, /device:TPU:8, one launch (start us, length us, event | category | flops | bytes accessed | tf_op | source)
XLA Modules:
  0.0 290.6 jit_solution(15201041775588603741)
XLA Ops:
  6.5 0.0 copy-start
  6.5 0.0 all-gather.5.cloned.1.call-start
  6.5 0.7 all-gather.5.cloned.1.call-update
  7.3 1.3 copy.27
  8.6 0.8 all_to_all.8
  9.4 11.4 %all-to-all-start = ((bf16[32,4,1176]{2,1,0:T(4,128)(2,1)}), bf16[32,4,1176]{2,1,0:T(4,128)(2,1)}, u32[]{:S(2)}, u32[]{:S(2)}) async-start(bf16[32,4,1176]{2,1,0:T(4,128)(2,1)} %all_to_all.8), calls=%async_computation | async-start | bytes 655360 | tf_op jit(solution)/shard_map/all_to_all | solution.py:97
  20.8 0.0 all-gather.7.cloned.1.call-start
  20.9 0.7 convert_reduce_fusion.1
  21.6 0.8 select_reduce_fusion.1
  22.4 0.1 fusion.26
  22.6 0.1 broadcast_multiply_fusion.1
  22.6 0.2 fusion.25
  22.8 0.9 mul.198
  23.7 2.2 copy.28
  25.9 8.5 %all-to-all-done = bf16[32,4,1176]{2,1,0:T(4,128)(2,1)} async-done(((bf16[32,4,1176]{2,1,0:T(4,128)(2,1)}), bf16[32,4,1176]{2,1,0:T(4,128)(2,1)}, u32[]{:S(2)}, u32[]{:S(2)}) %all-to-all-start) | async-done | bytes 301088 | tf_op jit(solution)/shard_map/all_to_all | solution.py:97
  34.4 1.1 all_to_all.10
  35.5 0.0 copy-done
  35.5 0.7 fusion.28
  36.2 0.0 copy-start.2
  36.2 0.8 copy-done.2
  37.1 0.2 multiply_reduce_fusion
  37.3 81.0 %all-gather.5.cloned.1.call-done = bf16[1280,3840]{1,0:T(8,128)(2,1)} async-done(((bf16[40,3840]{1,0:T(8,128)(2,1)}), bf16[1280,3840]{1,0:T(8,128)(2,1)}) %all-gather.5.cloned.1.call-update) | async-done | bytes 9830416 | tf_op jit(solution)/shard_map/all_gather | solution.py:109
  118.3 0.0 copy-done.4
  118.3 5.5 %convolution_add_fusion = f32[128,3840]{1,0:T(8,128)S(1)} fusion(bf16[1280,3840]{1,0:T(8,128)(2,1)} %all-gather.5.cloned.1.call-done, f32[3840]{0:T(1024)S(1)} %copy-done.7, f32[128,1280]{1,0:T(8,128)} %copy-done.2, f32[1280]{0:T(1024)S(1)} %copy-done.4, f32[1280]{0:T(1024)S(1)} %copy-done.5, f32[128]{0:T(128)S(1)} %add_rsqrt_fusion, ...), kind=kOutput, calls=%fused_computation.24 | convolution fusion | flops 1259601920 | bytes 12478464 | tf_op jit(solution)/shard_map/dot_general | solution.py:107
  123.8 1.3 copy-done.3
  125.1 1.1 fusion.27
  126.3 2.1 copy.29
  128.4 2.2 copy.32
  130.6 1.4 slice_negate_fusion
  131.9 1.2 maximum_multiply_fusion.1
  133.1 2.2 copy.30
  135.2 2.2 copy.33
  137.4 2.9 add_convert_fusion
  140.3 0.0 all-gather.7.cloned.1.call-update
  140.3 0.0 all-gather.9.cloned.1.call-start
  140.4 1.8 slice.41
  142.2 0.0 all-gather.9.cloned.1.call-update
  142.2 0.0 all-gather.11.cloned.1.call-start
  142.3 0.5 all-gather.11.cloned.1.call-update
  142.8 1.2 copy.34
  144.0 21.3 %all-gather.7.cloned.1.call-done = bf16[1024,1280]{1,0:T(8,128)(2,1)} async-done(((bf16[128,1280]{1,0:T(8,128)(2,1)}), bf16[1024,1280]{1,0:T(8,128)(2,1)}) %all-gather.7.cloned.1.call-update) | async-done | bytes 2621456 | tf_op jit(solution)/shard_map/all_gather | solution.py:140
  165.3 31.1 %all-gather.9.cloned.1.call-done = bf16[1024,1280]{1,0:T(8,128)(2,1)} async-done(((bf16[128,1280]{1,0:T(8,128)(2,1)}), bf16[1024,1280]{1,0:T(8,128)(2,1)}) %all-gather.9.cloned.1.call-update) | async-done | bytes 2621456 | tf_op jit(solution)/shard_map/all_gather | solution.py:141
  196.5 37.7 %while.20 = (s32[]{:T(128)}, f32[16,128]{1,0:T(8,128)S(1)}, f32[16,128]{1,0:T(8,128)S(1)}, f32[128,16,80]{0,2,1:T(8,128)}, s32[128]{0:T(128)S(1)}, /*index=5*/s3...) while((s32[]{:T(128)}, f32[16,128]{1,0:T(8,128)S(1)}, ...), condition=%wide.region_9.10_spmd.clone, body=%wide.region_5.9_spmd.clone.sunk | while | flops 349750272 | bytes 44511972 | solution.py:154
  196.5 3.5 %constant_dynamic-slice_fusion.3 = (bf16[512,1280]{1,0:T(8,128)(2,1)}, bf16[512,1280]{1,0:T(8,128)(2,1)}) fusion(bf16[1024,1280]{1,0:T(8,128)(2,1)} %get-tuple-element.432, s32[]{:T(128)S(6)} %select_n.85, bf16[1024,1280]{1,0:T(8,128)(2,1)} %get-tuple-element.430), kind=kLoop, calls=%fused_computation.19.clone.1 | loop fusion | bytes 5242884 | tf_op jit(solution)/shard_map/while/body/eval_jaxpr/dynamic_slice | solution.py:148
  199.9 2.4 copy.42
  202.4 0.1 convert_reduce_fusion.3
  202.5 0.1 broadcast_compare_fusion.2
  202.6 4.3 %fusion.50 = (f32[16,128]{1,0:T(8,128)S(1)}, f32[16,512,128]{2,1,0:T(8,128)}) fusion(pred[128,512]{0,1:T(8,128)(4,1)S(1)} %broadcast_compare_fusion.2, bf16[512,16,80]{0,2,1:T(8,128)(2,1)} %bitcast.64, bf16[128,16,80]{0,2,1:T(8,128)(2,1)S(1)} %get-tuple-element.431), kind=kOutput, calls=%fused_computation.2.clone.1 | convolution fusion | flops 170915840 | bytes 5906432 | tf_op jit(solution)/shard_map/while/body/eval_jaxpr/qhd,khd->hqk/dot_general | solution.py:61
  206.9 2.4 copy.43
  209.3 4.8 %fusion.54 = f32[128,16,80]{0,2,1:T(8,128)} fusion(bf16[512,16,80]{0,2,1:T(8,128)(2,1)} %bitcast.65, f32[16,512,128]{2,1,0:T(8,128)} %get-tuple-element.395, f32[16,128]{1,0:T(8,128)S(1)} %get-tuple-element.425, pred[128,512]{0,1:T(8,128)(4,1)S(1)} %broadcast_compare_fusion.2, f32[128,16,80]{0,2,1:T(8,128)} %get-tuple-element.414, ...), kind=kOutput, calls=%fused_computation.8.clone.1 | convolution fusion | flops 173506560 | bytes 6897665 | tf_op jit(solution)/shard_map/while/body/eval_jaxpr/hqk,khd->qhd/dot_general | solution.py:75
  214.2 0.0 copy-done.1
  214.2 1.0 fusion.52
  215.3 3.5 %constant_dynamic-slice_fusion.3 = (bf16[512,1280]{1,0:T(8,128)(2,1)}, bf16[512,1280]{1,0:T(8,128)(2,1)}) fusion(bf16[1024,1280]{1,0:T(8,128)(2,1)} %get-tuple-element.432, s32[]{:T(128)S(6)} %select_n.85, bf16[1024,1280]{1,0:T(8,128)(2,1)} %get-tuple-element.430), kind=kLoop, calls=%fused_computation.19.clone.1 | loop fusion | bytes 5242884 | tf_op jit(solution)/shard_map/while/body/eval_jaxpr/dynamic_slice | solution.py:148
  218.7 2.4 copy.42
  221.2 0.1 convert_reduce_fusion.3
  221.3 0.1 broadcast_compare_fusion.2
  221.4 4.3 %fusion.50 = (f32[16,128]{1,0:T(8,128)S(1)}, f32[16,512,128]{2,1,0:T(8,128)}) fusion(pred[128,512]{0,1:T(8,128)(4,1)S(1)} %broadcast_compare_fusion.2, bf16[512,16,80]{0,2,1:T(8,128)(2,1)} %bitcast.64, bf16[128,16,80]{0,2,1:T(8,128)(2,1)S(1)} %get-tuple-element.431), kind=kOutput, calls=%fused_computation.2.clone.1 | convolution fusion | flops 170915840 | bytes 5906432 | tf_op jit(solution)/shard_map/while/body/eval_jaxpr/qhd,khd->hqk/dot_general | solution.py:61
  225.7 2.4 copy.43
  228.1 5.0 %fusion.54 = f32[128,16,80]{0,2,1:T(8,128)} fusion(bf16[512,16,80]{0,2,1:T(8,128)(2,1)} %bitcast.65, f32[16,512,128]{2,1,0:T(8,128)} %get-tuple-element.395, f32[16,128]{1,0:T(8,128)S(1)} %get-tuple-element.425, pred[128,512]{0,1:T(8,128)(4,1)S(1)} %broadcast_compare_fusion.2, f32[128,16,80]{0,2,1:T(8,128)} %get-tuple-element.414, ...), kind=kOutput, calls=%fused_computation.8.clone.1 | convolution fusion | flops 173506560 | bytes 6897665 | tf_op jit(solution)/shard_map/while/body/eval_jaxpr/hqk,khd->qhd/dot_general | solution.py:75
  233.1 0.0 copy-done.1
  233.1 1.0 fusion.52
  234.2 1.1 divide_convert_fusion
  235.3 45.3 %all-gather.11.cloned.1.call-done = bf16[1280,1280]{1,0:T(8,128)(2,1)} async-done(((bf16[40,1280]{1,0:T(8,128)(2,1)}), bf16[1280,1280]{1,0:T(8,128)(2,1)}) %all-gather.11.cloned.1.call-update) | async-done | bytes 3276816 | tf_op jit(solution)/shard_map/all_gather | solution.py:163
  280.7 3.4 %fusion.18 = bf16[128,1280]{1,0:T(8,128)(2,1)} fusion(f32[128,1280]{1,0:T(8,128)} %copy-done.2, bf16[128,1280]{0,1:T(8,128)(2,1)S(1)} %bitcast.72, bf16[1280,1280]{1,0:T(8,128)(2,1)} %all-gather.11.cloned.1.call-done, f32[1280]{0:T(1024)S(1)} %copy-done.8), kind=kOutput, calls=%fused_computation.27 | convolution fusion | flops 419921920 | bytes 4592640 | tf_op jit(solution)/shard_map/dot_general | solution.py:161
  (31 shorter events, 0.1 us)
Async XLA Ops:
  6.5 29.0 %copy-start = (bf16[1176,1280]{1,0:T(8,128)(2,1)S(1)}, bf16[1176,1280]{1,0:T(8,128)(2,1)}, u32[]{:S(2)}) copy-start(bf16[1176,1280]{1,0:T(8,128)(2,1)} %param.13) | copy-start | bytes 9031684
  6.5 111.7 %all-gather.5.cloned.1.call-start = ((), (), s32[]{:S(2)}) async-start(), calls=%async_computation.1 | async-start | bytes 10137600 | tf_op jit(solution)/shard_map/all_gather | solution.py:109
  9.4 25.0 %all-to-all-start = ((bf16[32,4,1176]{2,1,0:T(4,128)(2,1)}), bf16[32,4,1176]{2,1,0:T(4,128)(2,1)}, u32[]{:S(2)}, u32[]{:S(2)}) async-start(bf16[32,4,1176]{2,1,0:T(4,128)(2,1)} %all_to_all.8), calls=%async_computation | async-start | bytes 655360 | tf_op jit(solution)/shard_map/all_to_all | solution.py:97
  20.8 144.5 %all-gather.7.cloned.1.call-start = ((), (), s32[]{:S(2)}) async-start(), calls=%async_computation.2 | async-start | bytes 2949120 | tf_op jit(solution)/shard_map/all_gather | solution.py:140
  23.7 94.6 %copy-start.4 = (f32[1280]{0:T(1024)S(1)}, f32[1280]{0:T(1024)}, u32[]{:S(2)}) copy-start(f32[1280]{0:T(1024)} %param.15) | copy-start | bytes 15364
  23.7 94.6 %copy-start.5 = (f32[1280]{0:T(1024)S(1)}, f32[1280]{0:T(1024)}, u32[]{:S(2)}) copy-start(f32[1280]{0:T(1024)} %param.14) | copy-start | bytes 15364
  23.7 94.6 %copy-start.7 = (f32[3840]{0:T(1024)S(1)}, f32[3840]{0:T(1024)}, u32[]{:S(2)}) copy-start(f32[3840]{0:T(1024)} %param.17) | copy-start | bytes 46084
  36.2 0.9 copy-start.2
  123.8 1.3 copy-start.3
  137.4 59.1 %copy-start.6 = (s32[1,3]{1,0:T(1,128)S(1)}, s32[1,3]{1,0:T(1,128)}, u32[]{:S(2)}) copy-start(s32[1,3]{1,0:T(1,128)} %param.20) | copy-start | bytes 40
  140.3 56.1 %all-gather.9.cloned.1.call-start = ((), (), s32[]{:S(2)}) async-start(), calls=%async_computation.3 | async-start | bytes 2949120 | tf_op jit(solution)/shard_map/all_gather | solution.py:141
  142.2 138.4 %all-gather.11.cloned.1.call-start = ((), (), s32[]{:S(2)}) async-start(), calls=%async_computation.4 | async-start | bytes 3379200 | tf_op jit(solution)/shard_map/all_gather | solution.py:163
  196.5 84.2 %copy-start.8 = (f32[1280]{0:T(1024)S(1)}, f32[1280]{0:T(1024)}, u32[]{:S(2)}) copy-start(f32[1280]{0:T(1024)} %param.19) | copy-start | bytes 15364
  209.3 4.9 %copy-start.1 = (f32[16,512,128]{2,1,0:T(8,128)S(1)}, f32[16,512,128]{2,1,0:T(8,128)}, u32[]{:S(2)}) copy-start(f32[16,512,128]{2,1,0:T(8,128)} %get-tuple-element.395) | copy-start | bytes 12582916 | tf_op jit(solution)/shard_map/while
  228.1 5.0 %copy-start.1 = (f32[16,512,128]{2,1,0:T(8,128)S(1)}, f32[16,512,128]{2,1,0:T(8,128)}, u32[]{:S(2)}) copy-start(f32[16,512,128]{2,1,0:T(8,128)} %get-tuple-element.395) | copy-start | bytes 12582916 | tf_op jit(solution)/shard_map/while
Sparse Core Ops, SparseCore 0:
  10.0 108.2 all-gather.4
  140.4 24.8 all-gather.6
  167.2 29.2 all-gather.8
  198.9 81.7 all-gather.10
where the time goes:
time: 291 us
  waiting for transfers between devices  188 us (65%)
  local copies, waits for them, and re-layouts  38 us (13%)
  matrix products  28.1 us (10%)
  between operations  13.3 us (5%)
  starting transfers between devices  11.6 us (4%)
  other arithmetic  11.2 us (4%)
    all_gather x1, waiting for transfers between devices, per_device(): lax.all_gather(qkv_weight, 'dp', axis=0, tiled=True)  81 us
    all_gather x1, waiting for transfers between devices, per_device(): lax.all_gather(out_weight, 'dp', axis=0, tiled=True)  45.3 us
    all_gather x1, waiting for transfers between devices, per_device(): piece_values = lax.all_gather(values, 'seq', axis=0, tiled=True)  31.1 us
    all_gather x1, waiting for transfers between devices, per_device(): piece_keys = lax.all_gather(key_rows, 'seq', axis=0, tiled=True)  21.3 us
    dynamic_slice x4, local copies, waits for them, and re-layouts, one_block(): value_block = lax.dynamic_slice_in_dim(piece_values, first_row, length, 0)  11.8 us
    all_to_all x1, starting transfers between devices, per_device(): lax.all_to_all(pixels, 'dp', split_axis=0, concat_axis=0, tiled=True)  11.4 us
    dot_general x2, matrix products, attend_block(): jnp.einsum('hqk,khd->qhd', weights.astype(jnp.bfloat16), value_block.resh...  9.84 us
    dot_general x2, matrix products, attend_block(): jnp.einsum('qhd,khd->hqk', queries3, key_block.reshape(count, HEADS, HDIM...  8.54 us
  transfers between devices with their start and end apart: 5, of which 5 were waited for; matrix products, arithmetic and copies ran while one was open for 17% of the time, Pallas kernels for 0%

commit v1 on v0

--- a/solution.py
+++ b/solution.py
@@ -137,7 +137,23 @@
         jnp.zeros((HEADS, tok_rows), jnp.float32),
         jnp.zeros((tok_rows, HEADS, HDIM), jnp.float32),
     )
-    piece_keys = lax.all_gather(key_rows, "seq", axis=0, tiled=True)
+
+    def proceed_the_masks(inputs, pos_dim):
+        n_blocks = lax.psum(1, axis_name="seq")
+        d_next = inputs
+        met_up = [(hop_no - 1, hop_no) for hop_no in range(1, n_blocks)] + [(n_blocks - 1, 0)]
+        items = [d_next]
+        for _ in range(n_blocks - 1):
+            d_next = lax.ppermute(d_next, axis_name="seq", perm=met_up)
+            items += [d_next]
+        base_arr = jnp.roll(
+            jnp.concatenate([*reversed(items)], axis=pos_dim),
+            shift=(lax.axis_index("seq") + 1) * d_next.shape[pos_dim],
+            axis=pos_dim,
+        )
+        return base_arr
+
+    piece_keys = proceed_the_masks(key_rows, 0)
     piece_values = lax.all_gather(values, "seq", axis=0, tiled=True)
     count = piece_keys.shape[0]
     length = block_length(count)

time: 291 us -> 288 us (0.990)
  waiting for transfers between devices: 188 us -> 169 us
  local copies, waits for them, and re-layouts: 38 us -> 53.6 us
    ppermute x0 -> x7, waiting for transfers between devices: none -> 44.6 us  [proceed_the_masks(): d_next = lax.ppermute(d_next, axis_name='seq', perm=met_up)]
    all_gather x1, waiting for transfers between devices: 31.1 us -> 0.01 us  [per_device(): piece_values = lax.all_gather(values, 'seq', axis=0, tiled=True)]
    all_gather x1 -> x0, waiting for transfers between devices: 21.3 us -> none  [per_device(): piece_keys = lax.all_gather(key_rows, 'seq', axis=0, tiled=True)]
    all_gather x1, waiting for transfers between devices: 45.3 us -> 31.2 us  [per_device(): lax.all_gather(out_weight, 'dp', axis=0, tiled=True)]
    unnamed x17 -> x56, local copies, waits for them, and re-layouts: 3.46 us -> 17.1 us
    all_to_all x1, waiting for transfers between devices: 8.46 us -> 11.9 us  [per_device(): lax.all_to_all(pixels, 'dp', split_axis=0, concat_axis=0, tiled=True)]
  transfers between devices with their start and end apart: 5 -> 11, of which waited for: 5 -> 10; matrix products, arithmetic and copies ran while one was open for 17% -> 26% of each run, Pallas kernels for 0% -> 0%
where the time goes in v1:
time: 288 us; the launch traced here: 287 us
  waiting for transfers between devices  169 us (59%)
  local copies, waits for them, and re-layouts  53.6 us (19%)
  matrix products  28 us (10%)
  between operations  13.5 us (5%)
  starting transfers between devices  11.6 us (4%)
  other arithmetic  11.2 us (4%)
    all_gather x1, waiting for transfers between devices, per_device(): lax.all_gather(qkv_weight, 'dp', axis=0, tiled=True)  80.9 us
    ppermute x7, waiting for transfers between devices, proceed_the_masks(): d_next = lax.ppermute(d_next, axis_name='seq', perm=met_up)  44.6 us
    all_gather x1, waiting for transfers between devices, per_device(): lax.all_gather(out_weight, 'dp', axis=0, tiled=True)  31.2 us
    unnamed x56, local copies, waits for them, and re-layouts  17.1 us
    all_to_all x1, waiting for transfers between devices, per_device(): lax.all_to_all(pixels, 'dp', split_axis=0, concat_axis=0, tiled=True)  11.9 us
    dynamic_slice x4, local copies, waits for them, and re-layouts, one_block(): value_block = lax.dynamic_slice_in_dim(piece_values, first_row, length, 0)  11.8 us
    all_to_all x1, starting transfers between devices, per_device(): lax.all_to_all(pixels, 'dp', split_axis=0, concat_axis=0, tiled=True)  11.4 us
    dot_general x2, matrix products, attend_block(): jnp.einsum('hqk,khd->qhd', weights.astype(jnp.bfloat16), value_block.resh...  9.84 us
  transfers between devices with their start and end apart: 11, of which 10 were waited for; matrix products, arithmetic and copies ran while one was open for 26% of the time, Pallas kernels for 0%

profile of v1, /device:TPU:8, one launch (start us, length us, event | category | flops | bytes accessed | tf_op | source)
XLA Modules:
  0.0 287.2 jit_solution(8920713215559462727)
XLA Ops:
  6.6 0.7 all-gather.4.cloned.1.call-update
  7.3 1.3 copy.27
  8.6 0.8 all_to_all.8
  9.4 11.4 %all-to-all-start = ((bf16[32,4,1176]{2,1,0:T(4,128)(2,1)}), bf16[32,4,1176]{2,1,0:T(4,128)(2,1)}, u32[]{:S(2)}, u32[]{:S(2)}) async-start(bf16[32,4,1176]{2,1,0:T(4,128)(2,1)} %all_to_all.8), calls=%async_computation | async-start | bytes 655360 | tf_op jit(solution)/shard_map/all_to_all | solution.py:97
  20.9 0.7 convert_reduce_fusion.1
  21.7 0.8 select_reduce_fusion.1
  22.6 11.9 %all-to-all-done = bf16[32,4,1176]{2,1,0:T(4,128)(2,1)} async-done(((bf16[32,4,1176]{2,1,0:T(4,128)(2,1)}), bf16[32,4,1176]{2,1,0:T(4,128)(2,1)}, u32[]{:S(2)}, u32[]{:S(2)}) %all-to-all-start) | async-done | bytes 301088 | tf_op jit(solution)/shard_map/all_to_all | solution.py:97
  34.4 1.1 all_to_all.10
  35.5 0.7 fusion.28
  36.3 0.9 copy-done.2
  37.4 80.9 %all-gather.4.cloned.1.call-done = bf16[1280,3840]{1,0:T(8,128)(2,1)} async-done(((bf16[40,3840]{1,0:T(8,128)(2,1)}), bf16[1280,3840]{1,0:T(8,128)(2,1)}) %all-gather.4.cloned.1.call-update) | async-done | bytes 9830416 | tf_op jit(solution)/shard_map/all_gather | solution.py:109
  118.2 5.5 %convolution_add_fusion = f32[128,3840]{1,0:T(8,128)S(1)} fusion(bf16[1280,3840]{1,0:T(8,128)(2,1)} %all-gather.4.cloned.1.call-done, f32[3840]{0:T(1024)S(1)} %copy-done.19, f32[128,1280]{1,0:T(8,128)} %copy-done.2, f32[1280]{0:T(1024)S(1)} %copy-done.16, f32[1280]{0:T(1024)S(1)} %copy-done.17, f32[128]{0:T(128)S(1)} %add_rsqrt_fusion, ...), kind=kOutput, calls=%fused_computation.24 | convolution fusion | flops 1259601920 | bytes 12478464 | tf_op jit(solution)/shard_map/dot_general | solution.py:107
  123.8 1.3 copy-done.3
  125.1 0.8 slice.41
  126.2 0.9 mul.201
  127.1 2.2 copy.28
  129.2 2.4 fusion.27
  131.7 2.2 copy.29
  133.9 2.2 copy.32
  136.1 1.4 slice_negate_fusion
  137.4 1.2 maximum_multiply_fusion.1
  138.6 2.2 copy.30
  140.8 2.2 copy.33
  143.0 2.8 add_convert_fusion
  145.8 0.7 copy-done.4
  146.5 6.5 %collective-permute-done = bf16[128,1280]{1,0:T(8,128)(2,1)S(1)} collective-permute-done((bf16[128,1280]{1,0:T(8,128)(2,1)S(1)}, bf16[128,1280]{1,0:T(8,128)(2,1)S(1)}, u32[]{:S(2)}, u32[]{:S(2)}) %collective-permute-start) | collective-permute-done | bytes 327712 | tf_op jit(solution)/shard_map/ppermute | solution.py:147
  153.0 0.7 copy-done.6
  153.7 6.5 %collective-permute-done.1 = bf16[128,1280]{1,0:T(8,128)(2,1)S(1)} collective-permute-done((bf16[128,1280]{1,0:T(8,128)(2,1)S(1)}, bf16[128,1280]{1,0:T(8,128)(2,1)S(1)}, u32[]{:S(2)}, u32[]{:S(2)}) %collective-permute-start.1) | collective-permute-done | bytes 327712 | tf_op jit(solution)/shard_map/ppermute | solution.py:147
  160.2 0.8 copy-done.8
  161.0 6.5 %collective-permute-done.2 = bf16[128,1280]{1,0:T(8,128)(2,1)S(1)} collective-permute-done((bf16[128,1280]{1,0:T(8,128)(2,1)S(1)}, bf16[128,1280]{1,0:T(8,128)(2,1)S(1)}, u32[]{:S(2)}, u32[]{:S(2)}) %collective-permute-start.2) | collective-permute-done | bytes 327712 | tf_op jit(solution)/shard_map/ppermute | solution.py:147
  167.5 0.7 copy-done.10
  168.2 6.5 %collective-permute-done.3 = bf16[128,1280]{1,0:T(8,128)(2,1)S(1)} collective-permute-done((bf16[128,1280]{1,0:T(8,128)(2,1)S(1)}, bf16[128,1280]{1,0:T(8,128)(2,1)S(1)}, u32[]{:S(2)}, u32[]{:S(2)}) %collective-permute-start.3) | collective-permute-done | bytes 327712 | tf_op jit(solution)/shard_map/ppermute | solution.py:147
  174.7 0.7 copy-done.12
  175.4 6.5 %collective-permute-done.4 = bf16[128,1280]{1,0:T(8,128)(2,1)S(1)} collective-permute-done((bf16[128,1280]{1,0:T(8,128)(2,1)S(1)}, bf16[128,1280]{1,0:T(8,128)(2,1)S(1)}, u32[]{:S(2)}, u32[]{:S(2)}) %collective-permute-start.4) | collective-permute-done | bytes 327712 | tf_op jit(solution)/shard_map/ppermute | solution.py:147
  181.9 0.7 copy-done.14
  182.7 6.6 %collective-permute-done.5 = bf16[128,1280]{1,0:T(8,128)(2,1)} collective-permute-done((bf16[128,1280]{1,0:T(8,128)(2,1)S(1)}, bf16[128,1280]{1,0:T(8,128)(2,1)}, u32[]{:S(2)}, u32[]{:S(2)}) %collective-permute-start.5) | collective-permute-done | bytes 327712 | tf_op jit(solution)/shard_map/ppermute | solution.py:147
  189.4 1.2 copy.34
  190.6 5.5 %collective-permute-done.6 = bf16[128,1280]{1,0:T(8,128)(2,1)} collective-permute-done((bf16[128,1280]{1,0:T(8,128)(2,1)}, bf16[128,1280]{1,0:T(8,128)(2,1)}, u32[]{:S(2)}, u32[]{:S(2)}) %collective-permute-start.6) | collective-permute-done | bytes 327712 | tf_op jit(solution)/shard_map/ppermute | solution.py:147
  196.1 1.0 constant_dynamic-update-slice_fusion.15
  197.1 1.0 constant_dynamic-update-slice_fusion.14
  198.1 1.0 constant_dynamic-update-slice_fusion.13
  199.1 1.0 constant_dynamic-update-slice_fusion.12
  200.1 1.0 constant_dynamic-update-slice_fusion.11
  201.1 1.0 constant_dynamic-update-slice_fusion.10
  202.1 1.0 constant_dynamic-update-slice_fusion.9
  203.2 1.0 constant_dynamic-update-slice_fusion.7
  204.2 1.0 constant_dynamic-update-slice_fusion.6
  205.4 1.7 constant_dynamic-slice_fusion.2
  207.1 37.7 %while.20 = (s32[]{:T(128)}, f32[16,128]{1,0:T(8,128)S(1)}, f32[16,128]{1,0:T(8,128)S(1)}, f32[128,16,80]{0,2,1:T(8,128)}, s32[128]{0:T(128)S(1)}, /*index=5*/s3...) while((s32[]{:T(128)}, f32[16,128]{1,0:T(8,128)S(1)}, ...), condition=%wide.region_9.10_spmd.clone, body=%wide.region_5.9_spmd.clone.sunk | while | flops 349750272 | bytes 44511972 | solution.py:170
  207.1 3.4 %constant_dynamic-slice_fusion.4 = (bf16[512,1280]{1,0:T(8,128)(2,1)}, bf16[512,1280]{1,0:T(8,128)(2,1)}) fusion(bf16[1024,1280]{1,0:T(8,128)(2,1)} %get-tuple-element.432, s32[]{:T(128)S(6)} %select_n.100, bf16[1024,1280]{1,0:T(8,128)(2,1)} %get-tuple-element.430), kind=kLoop, calls=%fused_computation.19.clone.1 | loop fusion | bytes 5242884 | tf_op jit(solution)/shard_map/while/body/eval_jaxpr/dynamic_slice | solution.py:164
  210.6 2.5 copy.42
  213.3 4.3 %fusion.50 = (f32[16,128]{1,0:T(8,128)S(1)}, f32[16,512,128]{2,1,0:T(8,128)}) fusion(pred[128,512]{0,1:T(8,128)(4,1)S(1)} %broadcast_compare_fusion.2, bf16[512,16,80]{0,2,1:T(8,128)(2,1)} %bitcast.64, bf16[128,16,80]{0,2,1:T(8,128)(2,1)S(1)} %get-tuple-element.431), kind=kOutput, calls=%fused_computation.2.clone.1 | convolution fusion | flops 170915840 | bytes 5906432 | tf_op jit(solution)/shard_map/while/body/eval_jaxpr/qhd,khd->hqk/dot_general | solution.py:61
  217.6 2.5 copy.43
  220.0 4.9 %fusion.54 = f32[128,16,80]{0,2,1:T(8,128)} fusion(bf16[512,16,80]{0,2,1:T(8,128)(2,1)} %bitcast.65, f32[16,512,128]{2,1,0:T(8,128)} %get-tuple-element.395, f32[16,128]{1,0:T(8,128)S(1)} %get-tuple-element.425, pred[128,512]{0,1:T(8,128)(4,1)S(1)} %broadcast_compare_fusion.2, f32[128,16,80]{0,2,1:T(8,128)} %get-tuple-element.414, ...), kind=kOutput, calls=%fused_computation.8.clone.1 | convolution fusion | flops 173506560 | bytes 6897665 | tf_op jit(solution)/shard_map/while/body/eval_jaxpr/hqk,khd->qhd/dot_general | solution.py:75
  224.9 1.0 fusion.52
  226.0 3.4 %constant_dynamic-slice_fusion.4 = (bf16[512,1280]{1,0:T(8,128)(2,1)}, bf16[512,1280]{1,0:T(8,128)(2,1)}) fusion(bf16[1024,1280]{1,0:T(8,128)(2,1)} %get-tuple-element.432, s32[]{:T(128)S(6)} %select_n.100, bf16[1024,1280]{1,0:T(8,128)(2,1)} %get-tuple-element.430), kind=kLoop, calls=%fused_computation.19.clone.1 | loop fusion | bytes 5242884 | tf_op jit(solution)/shard_map/while/body/eval_jaxpr/dynamic_slice | solution.py:164
  229.4 2.5 copy.42
  232.1 4.3 %fusion.50 = (f32[16,128]{1,0:T(8,128)S(1)}, f32[16,512,128]{2,1,0:T(8,128)}) fusion(pred[128,512]{0,1:T(8,128)(4,1)S(1)} %broadcast_compare_fusion.2, bf16[512,16,80]{0,2,1:T(8,128)(2,1)} %bitcast.64, bf16[128,16,80]{0,2,1:T(8,128)(2,1)S(1)} %get-tuple-element.431), kind=kOutput, calls=%fused_computation.2.clone.1 | convolution fusion | flops 170915840 | bytes 5906432 | tf_op jit(solution)/shard_map/while/body/eval_jaxpr/qhd,khd->hqk/dot_general | solution.py:61
  236.4 2.5 copy.43
  238.8 5.0 %fusion.54 = f32[128,16,80]{0,2,1:T(8,128)} fusion(bf16[512,16,80]{0,2,1:T(8,128)(2,1)} %bitcast.65, f32[16,512,128]{2,1,0:T(8,128)} %get-tuple-element.395, f32[16,128]{1,0:T(8,128)S(1)} %get-tuple-element.425, pred[128,512]{0,1:T(8,128)(4,1)S(1)} %broadcast_compare_fusion.2, f32[128,16,80]{0,2,1:T(8,128)} %get-tuple-element.414, ...), kind=kOutput, calls=%fused_computation.8.clone.1 | convolution fusion | flops 173506560 | bytes 6897665 | tf_op jit(solution)/shard_map/while/body/eval_jaxpr/hqk,khd->qhd/dot_general | solution.py:75
  243.8 1.0 fusion.52
  244.9 1.1 divide_convert_fusion
  246.0 31.2 %all-gather.8.cloned.1.call-done = bf16[1280,1280]{1,0:T(8,128)(2,1)} async-done(((bf16[40,1280]{1,0:T(8,128)(2,1)}), bf16[1280,1280]{1,0:T(8,128)(2,1)}) %all-gather.8.cloned.1.call-update) | async-done | bytes 3276816 | tf_op jit(solution)/shard_map/all_gather | solution.py:179
  277.2 3.4 %fusion.18 = bf16[128,1280]{1,0:T(8,128)(2,1)} fusion(f32[128,1280]{1,0:T(8,128)} %copy-done.2, bf16[128,1280]{0,1:T(8,128)(2,1)S(1)} %bitcast.72, bf16[1280,1280]{1,0:T(8,128)(2,1)} %all-gather.8.cloned.1.call-done, f32[1280]{0:T(1024)S(1)} %copy-done.20), kind=kOutput, calls=%fused_computation.27 | convolution fusion | flops 419921920 | bytes 4592640 | tf_op jit(solution)/shard_map/dot_general | solution.py:177
  (83 shorter events, 1.5 us)
Async XLA Ops:
  6.5 29.0 %copy-start = (bf16[1176,1280]{1,0:T(8,128)(2,1)S(1)}, bf16[1176,1280]{1,0:T(8,128)(2,1)}, u32[]{:S(2)}) copy-start(bf16[1176,1280]{1,0:T(8,128)(2,1)} %param.13) | copy-start | bytes 9031684
  6.5 111.7 %copy-start.17 = (f32[1280]{0:T(1024)S(1)}, f32[1280]{0:T(1024)}, u32[]{:S(2)}) copy-start(f32[1280]{0:T(1024)} %param.14) | copy-start | bytes 15364
  6.5 111.7 %copy-start.16 = (f32[1280]{0:T(1024)S(1)}, f32[1280]{0:T(1024)}, u32[]{:S(2)}) copy-start(f32[1280]{0:T(1024)} %param.15) | copy-start | bytes 15364
  6.5 111.7 %copy-start.19 = (f32[3840]{0:T(1024)S(1)}, f32[3840]{0:T(1024)}, u32[]{:S(2)}) copy-start(f32[3840]{0:T(1024)} %param.17) | copy-start | bytes 46084
  6.5 111.7 %all-gather.4.cloned.1.call-start = ((), (), s32[]{:S(2)}) async-start(), calls=%async_computation.1 | async-start | bytes 10137600 | tf_op jit(solution)/shard_map/all_gather | solution.py:109
  9.4 25.0 %all-to-all-start = ((bf16[32,4,1176]{2,1,0:T(4,128)(2,1)}), bf16[32,4,1176]{2,1,0:T(4,128)(2,1)}, u32[]{:S(2)}, u32[]{:S(2)}) async-start(bf16[32,4,1176]{2,1,0:T(4,128)(2,1)} %all_to_all.8), calls=%async_computation | async-start | bytes 655360 | tf_op jit(solution)/shard_map/all_to_all | solution.py:97
  20.9 186.3 %all-gather.6.cloned.1.call-start = ((), (), s32[]{:S(2)}) async-start(), calls=%async_computation.2 | async-start | bytes 2949120 | tf_op jit(solution)/shard_map/all_gather | solution.py:157
  36.3 0.9 copy-start.2
  123.8 1.3 copy-start.3
  125.9 151.4 %all-gather.8.cloned.1.call-start = ((), (), s32[]{:S(2)}) async-start(), calls=%async_computation.3 | async-start | bytes 3379200 | tf_op jit(solution)/shard_map/all_gather | solution.py:179
  145.8 0.7 copy-start.4
  146.5 6.5 %collective-permute-start = (bf16[128,1280]{1,0:T(8,128)(2,1)S(1)}, bf16[128,1280]{1,0:T(8,128)(2,1)S(1)}, u32[]{:S(2)}, u32[]{:S(2)}) collective-permute-start(bf16[128,1280]{1,0:T(8,128)(2,1)S(1)} %get-tuple-element.314), channel_id=1, source_target_pairs={{0,1},{1,2},{2,3},{3,4},{4,5},{5,6},{6,7},{7,0},{8,9},{9,10},{10,1... | collective-permute-start | bytes 983048 | tf_op jit(solution)/shard_map/ppermute | solution.py:147
  153.0 0.7 copy-start.6
  153.7 6.5 %collective-permute-start.1 = (bf16[128,1280]{1,0:T(8,128)(2,1)S(1)}, bf16[128,1280]{1,0:T(8,128)(2,1)S(1)}, u32[]{:S(2)}, u32[]{:S(2)}) collective-permute-start(bf16[128,1280]{1,0:T(8,128)(2,1)S(1)} %collective-permute-done), channel_id=1, source_target_pairs={{0,1},{1,2},{2,3},{3,4},{4,5},{5,6},{6,7},{7,0},{8,9},{9,10},{10,1... | collective-permute-start | bytes 983048 | tf_op jit(solution)/shard_map/ppermute | solution.py:147
  160.2 0.8 copy-start.8
  161.0 6.5 %collective-permute-start.2 = (bf16[128,1280]{1,0:T(8,128)(2,1)S(1)}, bf16[128,1280]{1,0:T(8,128)(2,1)S(1)}, u32[]{:S(2)}, u32[]{:S(2)}) collective-permute-start(bf16[128,1280]{1,0:T(8,128)(2,1)S(1)} %collective-permute-done.1), channel_id=1, source_target_pairs={{0,1},{1,2},{2,3},{3,4},{4,5},{5,6},{6,7},{7,0},{8,9},{9,10},{10,1... | collective-permute-start | bytes 983048 | tf_op jit(solution)/shard_map/ppermute | solution.py:147
  167.5 0.7 copy-start.10
  168.2 6.5 %collective-permute-start.3 = (bf16[128,1280]{1,0:T(8,128)(2,1)S(1)}, bf16[128,1280]{1,0:T(8,128)(2,1)S(1)}, u32[]{:S(2)}, u32[]{:S(2)}) collective-permute-start(bf16[128,1280]{1,0:T(8,128)(2,1)S(1)} %collective-permute-done.2), channel_id=1, source_target_pairs={{0,1},{1,2},{2,3},{3,4},{4,5},{5,6},{6,7},{7,0},{8,9},{9,10},{10,1... | collective-permute-start | bytes 983048 | tf_op jit(solution)/shard_map/ppermute | solution.py:147
  174.7 0.7 copy-start.12
  175.4 6.5 %collective-permute-start.4 = (bf16[128,1280]{1,0:T(8,128)(2,1)S(1)}, bf16[128,1280]{1,0:T(8,128)(2,1)S(1)}, u32[]{:S(2)}, u32[]{:S(2)}) collective-permute-start(bf16[128,1280]{1,0:T(8,128)(2,1)S(1)} %collective-permute-done.3), channel_id=1, source_target_pairs={{0,1},{1,2},{2,3},{3,4},{4,5},{5,6},{6,7},{7,0},{8,9},{9,10},{10,1... | collective-permute-start | bytes 983048 | tf_op jit(solution)/shard_map/ppermute | solution.py:147
  181.9 0.7 copy-start.14
  182.7 6.6 %collective-permute-start.5 = (bf16[128,1280]{1,0:T(8,128)(2,1)S(1)}, bf16[128,1280]{1,0:T(8,128)(2,1)}, u32[]{:S(2)}, u32[]{:S(2)}) collective-permute-start(bf16[128,1280]{1,0:T(8,128)(2,1)S(1)} %collective-permute-done.4), channel_id=1, source_target_pairs={{0,1},{1,2},{2,3},{3,4},{4,5},{5,6},{6,7},{7,0},{8,9},{9,10},{10,1... | collective-permute-start | bytes 983048 | tf_op jit(solution)/shard_map/ppermute | solution.py:147
  189.3 6.8 %collective-permute-start.6 = (bf16[128,1280]{1,0:T(8,128)(2,1)}, bf16[128,1280]{1,0:T(8,128)(2,1)}, u32[]{:S(2)}, u32[]{:S(2)}) collective-permute-start(bf16[128,1280]{1,0:T(8,128)(2,1)} %collective-permute-done.5), channel_id=1, source_target_pairs={{0,1},{1,2},{2,3},{3,4},{4,5},{5,6},{6,7},{7,0},{8,9},{9,10},{10,1... | collective-permute-start | bytes 983048 | tf_op jit(solution)/shard_map/ppermute | solution.py:147
  190.5 12.6 %copy-start.5 = (bf16[128,1280]{1,0:T(8,128)(2,1)S(1)}, bf16[128,1280]{1,0:T(8,128)(2,1)}, u32[]{:S(2)}) copy-start(bf16[128,1280]{1,0:T(8,128)(2,1)} %copy-done.4) | copy-start | bytes 983044
  190.5 14.6 %copy-start.15 = (bf16[128,1280]{1,0:T(8,128)(2,1)S(1)}, bf16[128,1280]{1,0:T(8,128)(2,1)}, u32[]{:S(2)}) copy-start(bf16[128,1280]{1,0:T(8,128)(2,1)} %copy-done.14) | copy-start | bytes 983044
  190.6 14.7 %copy-start.13 = (bf16[128,1280]{1,0:T(8,128)(2,1)S(1)}, bf16[128,1280]{1,0:T(8,128)(2,1)}, u32[]{:S(2)}) copy-start(bf16[128,1280]{1,0:T(8,128)(2,1)} %copy-done.12) | copy-start | bytes 983044
  190.6 14.7 %copy-start.11 = (bf16[128,1280]{1,0:T(8,128)(2,1)S(1)}, bf16[128,1280]{1,0:T(8,128)(2,1)}, u32[]{:S(2)}) copy-start(bf16[128,1280]{1,0:T(8,128)(2,1)} %copy-done.10) | copy-start | bytes 983044
  190.6 14.7 %copy-start.9 = (bf16[128,1280]{1,0:T(8,128)(2,1)S(1)}, bf16[128,1280]{1,0:T(8,128)(2,1)}, u32[]{:S(2)}) copy-start(bf16[128,1280]{1,0:T(8,128)(2,1)} %copy-done.8) | copy-start | bytes 983044
  197.1 8.3 %copy-start.7 = (bf16[128,1280]{1,0:T(8,128)(2,1)S(1)}, bf16[128,1280]{1,0:T(8,128)(2,1)}, u32[]{:S(2)}) copy-start(bf16[128,1280]{1,0:T(8,128)(2,1)} %copy-done.6) | copy-start | bytes 983044
  205.2 1.9 copy-start.18
  207.1 70.1 %copy-start.20 = (f32[1280]{0:T(1024)S(1)}, f32[1280]{0:T(1024)}, u32[]{:S(2)}) copy-start(f32[1280]{0:T(1024)} %param.19) | copy-start | bytes 15364
  220.0 4.9 %copy-start.1 = (f32[16,512,128]{2,1,0:T(8,128)S(1)}, f32[16,512,128]{2,1,0:T(8,128)}, u32[]{:S(2)}) copy-start(f32[16,512,128]{2,1,0:T(8,128)} %get-tuple-element.395) | copy-start | bytes 12582916 | tf_op jit(solution)/shard_map/while
  238.8 5.0 %copy-start.1 = (f32[16,512,128]{2,1,0:T(8,128)S(1)}, f32[16,512,128]{2,1,0:T(8,128)}, u32[]{:S(2)}) copy-start(f32[16,512,128]{2,1,0:T(8,128)} %get-tuple-element.395) | copy-start | bytes 12582916 | tf_op jit(solution)/shard_map/while
Sparse Core Ops, SparseCore 0:
  10.0 108.2 all-gather.3
  126.0 24.8 all-gather.5
  189.4 87.7 all-gather.7
